TPU v7x, 32 devices: a whole 2x2x4 slice. The times are simulated.
32 devices in a mesh: ctx: 8 (over y, x, core), ch: 4 (over z).
Axes of the slice: x: 2, y: 2, z: 4, core: 2. Of those that a mesh axis runs over, the one named last changes fastest.
Arguments:
- queries: bfloat16 [1024, 4096], P('ctx', 'ch'), may hold values from -6 to 6
- keys: bfloat16 [1024, 4096], P('ctx', 'ch'), may hold values from -6 to 6
- values: bfloat16 [1024, 4096], P('ctx', 'ch'), may hold values from -6 to 6
- grad_out: bfloat16 [1024, 4096], P('ctx', 'ch'), may hold values from -6 to 6
- residues: float32 [4096, 16], P('ch'), may hold values from -0.1875 to 0.1875
- decays: float32 [4096, 16], P('ch'), may hold values from 0.0009765625 to 0.03
- skip: float32 [4096], P('ch'), may hold values from -6 to 6
Outputs:
- query_grad: bfloat16 [1024, 4096], P('ctx', 'ch')
- key_grad: bfloat16 [1024, 4096], P('ctx', 'ch')
- value_grad: bfloat16 [1024, 4096], P('ctx', 'ch')
- residue_grad: float32 [4096, 16], P('ch')
- decay_grad: float32 [4096, 16], P('ch')
All inputs are finite; a program needn't handle non-finite values.
Results may differ from a plain program's by a relative error of at most 0.001.
Values sent between devices are 32-bit elements; how exact they have to be, the bound alone decides.
A program may use at most 128 MiB of HBM per device.

v0:
```python
import functools

import jax
import jax.numpy as jnp
from jax import lax
from jax.experimental import pallas as pl
from jax.experimental.pallas import tpu as pltpu
from jax.sharding import PartitionSpec as P

LANES = 128
SUB = 8
MESH = pl.DeviceIdType.MESH
f32 = jnp.float32


def kernel(
    n, own, q_ref, k_ref, v_ref, g_ref, res_ref, dec_ref, skip_ref,
    qg_ref, kg_ref, vg_ref, rg_ref, dg_ref,
    u_s, o_s, conv_s, adj_s, d_s, a_s, w_s, rt_s, dt_s, send1, got1, send2, got2,
    ss1, rs1, ss2, rs2,
):
    rows, cols = q_ref.shape
    modes = res_ref.shape[1]
    groups = cols // LANES
    seq = rows * n
    slab = modes * groups // own
    per = slab // SUB
    me = lax.axis_index("ctx")

    barrier = pltpu.get_barrier_semaphore()

    @pl.loop(0, n)
    def _(peer):
        @pl.when(peer != me)
        def _():
            pl.semaphore_signal(barrier, inc=1, device_id={"ctx": peer}, device_id_type=MESH)

    for g in range(groups):
        lanes = slice(g * LANES, (g + 1) * LANES)
        block = slice(g * rows, (g + 1) * rows)
        u = k_ref[:, lanes].astype(f32) * v_ref[:, lanes].astype(f32)
        o = q_ref[:, lanes].astype(f32) * g_ref[:, lanes].astype(f32)
        skip = skip_ref[:, lanes]
        u_s[block, :] = u
        o_s[block, :] = o
        conv_s[block, :] = skip * u
        adj_s[block, :] = skip * o
        d = dec_ref[lanes, :].T
        d_s[pl.ds(g, modes, stride=groups), :] = d
        a_s[pl.ds(g, modes, stride=groups), :] = jnp.exp(-d)
        w_s[pl.ds(g, modes, stride=groups), :] = res_ref[lanes, :].T

    def at(ref, t):
        return ref.at[pl.ds(t, SUB, stride=rows), :]

    def mode_rows(m):
        return pl.ds(pl.multiple_of(m * SUB, SUB), SUB)

    pl.semaphore_wait(barrier, n - 1)

    zero = jnp.zeros((SUB, LANES), f32)
    batch = 4
    turns = modes // batch
    owners_per = batch // per
    unroll = 8

    def to_owner(q):
        return pltpu.make_async_remote_copy(
            src_ref=send1.at[q], dst_ref=got1.at[me], send_sem=ss1.at[q], recv_sem=rs1.at[me],
            device_id={"ctx": q}, device_id_type=MESH)

    @pl.loop(0, turns)
    def _(turn):
        c = lax.rem(turn + me // owners_per, turns)
        a = [a_s[mode_rows(c * batch + j), :] for j in range(batch)]

        def step(i, carry):
            x, y, r, e, z, v = [list(s) for s in carry]
            for k in range(unroll):
                t = i * unroll + k
                ut = at(u_s, t)[...]
                ot = at(o_s, t)[...]
                ob = at(o_s, rows - 1 - t)[...]
                for j in range(batch):
                    y[j] = a[j] * (y[j] + x[j])
                    x[j] = a[j] * x[j] + ut
                    r[j] = r[j] + ot * x[j]
                    e[j] = e[j] + ot * y[j]
                    z[j] = a[j] * z[j] + ob
                    v[j] = a[j] * v[j] + z[j]
            return tuple(tuple(s) for s in (x, y, r, e, z, v))

        done = lax.fori_loop(0, rows // unroll, step, tuple((zero,) * batch for _ in range(6)))
        for j in range(batch):
            for f in range(6):
                send1[c * owners_per + j // per, f, (j % per) * SUB:(j % per + 1) * SUB, :] = done[f][j]
        for b in range(owners_per):
            q = c * owners_per + b

            @pl.when(q != me)
            def _():
                to_owner(q).start()

    batch2 = 8

    @pl.loop(0, modes // batch2)
    def _(c):
        a = [a_s[mode_rows(c * batch2 + j), :] for j in range(batch2)]
        w = [w_s[mode_rows(c * batch2 + j), :] for j in range(batch2)]

        def step(i, carry):
            x, z = [list(s) for s in carry]
            for k in range(unroll):
                t = i * unroll + k
                b = rows - 1 - t
                ut = at(u_s, t)[...]
                ob = at(o_s, b)[...]
                cs = []
                zs = []
                for j in range(batch2):
                    x[j] = a[j] * x[j] + ut
                    z[j] = a[j] * z[j] + ob
                    cs.append(w[j] * x[j])
                    zs.append(w[j] * z[j])
                while len(cs) > 1:
                    cs = [p + q for p, q in zip(cs[::2], cs[1::2])]
                    zs = [p + q for p, q in zip(zs[::2], zs[1::2])]
                at(conv_s, t)[...] = at(conv_s, t)[...] + cs[0]
                at(adj_s, b)[...] = at(adj_s, b)[...] + zs[0]
            return tuple(x), tuple(z)

        lax.fori_loop(0, rows // unroll, step, ((zero,) * batch2, (zero,) * batch2))

    def from_peer(r):
        return pltpu.make_async_remote_copy(
            src_ref=send1.at[0], dst_ref=got1.at[r], send_sem=ss1.at[0], recv_sem=rs1.at[r],
            device_id={"ctx": r}, device_id_type=MESH)

    def back(r):
        return pltpu.make_async_remote_copy(
            src_ref=send2.at[r], dst_ref=got2.at[me], send_sem=ss2.at[r], recv_sem=rs2.at[me],
            device_id={"ctx": r}, device_id_type=MESH)

    def from_owner(q):
        return pltpu.make_async_remote_copy(
            src_ref=send2.at[0], dst_ref=got2.at[q], send_sem=ss2.at[0], recv_sem=rs2.at[q],
            device_id={"ctx": q}, device_id_type=MESH)

    @pl.when(me < own)
    def _():
        got1[me] = send1[me]

        @pl.loop(0, n)
        def _(r):
            @pl.when(r != me)
            def _():
                from_peer(r).wait_recv()

        mine = pl.ds(pl.multiple_of(me * slab, slab), slab)
        d = d_s[mine, :]
        a = a_s[mine, :]
        at_end = jnp.exp(-float(rows) * d)
        none = jnp.zeros((slab, LANES), f32)

        def ahead(r, carry):
            x, y, rt, dt = carry
            send2[r, 0] = x
            z, v = got1[r, 4], got1[r, 5]
            rt = rt + got1[r, 2] + a * (x * z)
            dt = dt + got1[r, 3] + a * (v * x + z * y)
            y = at_end * (y + float(rows) * x) + got1[r, 1]
            x = at_end * x + got1[r, 0]
            return x, y, rt, dt

        few = n <= 16
        _, _, rt, dt = lax.fori_loop(0, n, ahead, (none,) * 4, unroll=few)
        rt = rt / seq
        dt = dt * d / seq

        def behind(i, z):
            r = n - 1 - i
            send2[r, 1] = z
            send2[r, 2] = rt
            send2[r, 3] = dt
            z = at_end * z + got1[r, 4]
            return z

        lax.fori_loop(0, n, behind, none, unroll=few)

        @pl.loop(0, n)
        def _(r):
            @pl.when(r != me)
            def _():
                back(r).start()

        got2[me] = send2[me]

    @pl.loop(0, own)
    def _(q):
        @pl.when(q != me)
        def _():
            from_owner(q).wait_recv()

    @pl.loop(0, modes // batch2)
    def _(c):
        a, p, s = [], [], []
        for j in range(batch2):
            m = c * batch2 + j
            aj = a_s[mode_rows(m), :]
            wa = w_s[mode_rows(m), :] * aj
            q = m // per
            sub = pl.ds(pl.multiple_of((m % per) * SUB, SUB), SUB)
            a.append(aj)
            p.append(wa * got2[q, 0, sub, :])
            s.append(wa * got2[q, 1, sub, :])
            rt_s[mode_rows(m), :] = got2[q, 2, sub, :]
            dt_s[mode_rows(m), :] = got2[q, 3, sub, :]

        def step(i, carry):
            p, s = [list(x) for x in carry]
            for k in range(unroll):
                t = i * unroll + k
                b = rows - 1 - t
                cs, zs = list(p), list(s)
                while len(cs) > 1:
                    cs = [x + y for x, y in zip(cs[::2], cs[1::2])]
                    zs = [x + y for x, y in zip(zs[::2], zs[1::2])]
                at(conv_s, t)[...] = at(conv_s, t)[...] + cs[0]
                at(adj_s, b)[...] = at(adj_s, b)[...] + zs[0]
                p = [x * y for x, y in zip(a, p)]
                s = [x * y for x, y in zip(a, s)]
            return tuple(p), tuple(s)

        lax.fori_loop(0, rows // unroll, step, (tuple(p), tuple(s)))

    for g in range(groups):
        lanes = slice(g * LANES, (g + 1) * LANES)
        block = slice(g * rows, (g + 1) * rows)
        adj = adj_s[block, :]
        qg_ref[:, lanes] = (g_ref[:, lanes].astype(f32) * conv_s[block, :]).astype(qg_ref.dtype)
        kg_ref[:, lanes] = (adj * v_ref[:, lanes].astype(f32)).astype(kg_ref.dtype)
        vg_ref[:, lanes] = (adj * k_ref[:, lanes].astype(f32)).astype(vg_ref.dtype)
        rg_ref[lanes, :] = rt_s[pl.ds(g, modes, stride=groups), :].T
        dg_ref[lanes, :] = dt_s[pl.ds(g, modes, stride=groups), :].T

    @pl.loop(0, own)
    def _(q):
        @pl.when(q != me)
        def _():
            to_owner(q).wait_send()

    @pl.when(me < own)
    def _():
        @pl.loop(0, n)
        def _(r):
            @pl.when(r != me)
            def _():
                back(r).wait_send()


def body(n, queries, keys, values, grad_out, residues, decays, skip):
    rows, cols = queries.shape
    modes = residues.shape[1]
    own = min(n, modes)
    slab = modes * cols // LANES // own
    vmem = pl.BlockSpec(memory_space=pltpu.VMEM)
    field = pltpu.VMEM((rows * cols // LANES, LANES), f32)
    table = pltpu.VMEM((modes * cols // LANES, LANES), f32)
    grads = jax.ShapeDtypeStruct((rows, cols), jnp.bfloat16)
    sums = jax.ShapeDtypeStruct((cols, modes), f32)
    return pl.pallas_call(
        functools.partial(kernel, n, own),
        out_shape=(grads, grads, grads, sums, sums),
        in_specs=[vmem] * 7,
        out_specs=(vmem,) * 5,
        scratch_shapes=[
            field, field, field, field,
            table, table, table, table, table,
            pltpu.VMEM((own, 6, slab, LANES), f32),
            pltpu.VMEM((n, 6, slab, LANES), f32),
            pltpu.VMEM((n, 4, slab, LANES), f32),
            pltpu.VMEM((own, 4, slab, LANES), f32),
            pltpu.SemaphoreType.DMA((own,)),
            pltpu.SemaphoreType.DMA((n,)),
            pltpu.SemaphoreType.DMA((n,)),
            pltpu.SemaphoreType.DMA((own,)),
        ],
        compiler_params=pltpu.CompilerParams(
            collective_id=0, has_side_effects=True, vmem_limit_bytes=40 * 1024 * 1024
        ),
    )(queries, keys, values, grad_out, residues, decays, skip.reshape(1, cols))


def solution(mesh):
    return jax.shard_map(
        functools.partial(body, mesh.shape["ctx"]),
        mesh=mesh,
        in_specs=(
            P("ctx", "ch"), P("ctx", "ch"), P("ctx", "ch"), P("ctx", "ch"),
            P("ch", None), P("ch", None), P("ch"),
        ),
        out_specs=(P("ctx", "ch"), P("ctx", "ch"), P("ctx", "ch"), P("ch", None), P("ch", None)),
        check_vma=False,
    )
```

profile of v0, /device:TPU:0, one launch (start us, length us, event | category | flops | bytes accessed | tf_op | source)
XLA Modules:
  0.0 30.8 jit_solution(9797622017291251996)
XLA Ops:
  0.6 0.0 copy-start.5
  0.6 1.1 %copy.12.res_ref = f32[1024,16]{1,0:T(8,128)S(1)} copy(f32[1024,16]{0,1:T(8,128)} %param.11) | data formatting | bytes 131072 | tf_op args[4]
  1.7 0.0 copy-done.5
  1.7 0.0 copy-start
  1.7 0.0 copy-start.1
  1.7 0.0 copy-start.4
  1.8 0.2 copy.13.dec_ref
  2.0 0.7 %copy-done = bf16[128,1024]{1,0:T(8,128)(2,1)S(1)} copy-done((bf16[128,1024]{1,0:T(8,128)(2,1)S(1)}, bf16[128,1024]{1,0:T(8,128)(2,1)}, u32[]{:S(2)}) %copy-start) | copy-done | bytes 262168
  2.7 0.1 copy-done.1
  2.8 0.0 copy-done.4
  2.8 0.0 copy-start.2
  2.8 0.9 %copy-done.2 = bf16[128,1024]{1,0:T(8,128)(2,1)S(1)} copy-done((bf16[128,1024]{1,0:T(8,128)(2,1)S(1)}, bf16[128,1024]{1,0:T(8,128)(2,1)}, u32[]{:S(2)}) %copy-start.2) | copy-done | bytes 262168
  3.7 0.0 copy-start.3
  3.7 0.9 %copy-done.3 = bf16[128,1024]{1,0:T(8,128)(2,1)S(1)} copy-done((bf16[128,1024]{1,0:T(8,128)(2,1)S(1)}, bf16[128,1024]{1,0:T(8,128)(2,1)}, u32[]{:S(2)}) %copy-start.3) | copy-done | bytes 262168
  4.7 22.4 %shard_map.110 = (bf16[128,1024]{1,0:T(8,128)(2,1)S(1)}, bf16[128,1024]{1,0:T(8,128)(2,1)S(1)}, bf16[128,1024]{1,0:T(8,128)(2,1)S(1)}, f32[1024,16]{1,0:T(8,128)S(1)}, f32[1024,16]{1,0:T(8,128)S(1)}) custom-call(bf16[128,1024]{1,0:T(8,128)(2,1)S(1)} %copy-done, bf16[128,1024]{1,0:T(8,128)(2,1)S(1)} %copy-done.1, bf16[128,1024]{1,0:T(8,128)(2,1)S(1)} %copy-done.2, ...), custom_call_target="tpu_custom_call" | custom-call | tf_op jit(solution)/shard_map/pallas_call | solution.py:271
  27.1 0.8 %copy.14 = f32[1024,16]{0,1:T(8,128)} copy(f32[1024,16]{1,0:T(8,128)S(1)} %get-tuple-element.8) | data formatting | bytes 131072 | tf_op jit(solution)/shard_map/pallas_call | solution.py:271
  27.9 0.8 %copy.15 = f32[1024,16]{0,1:T(8,128)} copy(f32[1024,16]{1,0:T(8,128)S(1)} %get-tuple-element.9) | data formatting | bytes 131072 | tf_op jit(solution)/shard_map/pallas_call | solution.py:271
  28.7 0.7 %copy.19 = bf16[128,1024]{1,0:T(8,128)(2,1)} copy(bf16[128,1024]{1,0:T(8,128)(2,1)S(1)} %get-tuple-element.15) | data formatting | bytes 524288
  29.4 0.7 %copy.20 = bf16[128,1024]{1,0:T(8,128)(2,1)} copy(bf16[128,1024]{1,0:T(8,128)(2,1)S(1)} %get-tuple-element.16) | data formatting | bytes 524288
  30.1 0.7 %copy.21 = bf16[128,1024]{1,0:T(8,128)(2,1)} copy(bf16[128,1024]{1,0:T(8,128)(2,1)S(1)} %get-tuple-element.17) | data formatting | bytes 524288
Async XLA Ops:
  0.6 1.1 %copy-start.5 = (f32[1024,16]{0,1:T(8,128)S(1)}, f32[1024,16]{0,1:T(8,128)}, u32[]{:S(2)}) copy-start(f32[1024,16]{0,1:T(8,128)} %param.12) | copy-start | bytes 196612
  1.7 1.0 %copy-start = (bf16[128,1024]{1,0:T(8,128)(2,1)S(1)}, bf16[128,1024]{1,0:T(8,128)(2,1)}, u32[]{:S(2)}) copy-start(bf16[128,1024]{1,0:T(8,128)(2,1)} %q_ref.1) | copy-start | bytes 786436
  1.7 1.0 %copy-start.1 = (bf16[128,1024]{1,0:T(8,128)(2,1)S(1)}, bf16[128,1024]{1,0:T(8,128)(2,1)}, u32[]{:S(2)}) copy-start(bf16[128,1024]{1,0:T(8,128)(2,1)} %k_ref.1) | copy-start | bytes 786436
  1.7 1.0 %copy-start.4 = (f32[1024]{0:T(1024)S(1)}, f32[1024]{0:T(1024)}, u32[]{:S(2)}) copy-start(f32[1024]{0:T(1024)} %param.13) | copy-start | bytes 12292
  2.8 1.0 %copy-start.2 = (bf16[128,1024]{1,0:T(8,128)(2,1)S(1)}, bf16[128,1024]{1,0:T(8,128)(2,1)}, u32[]{:S(2)}) copy-start(bf16[128,1024]{1,0:T(8,128)(2,1)} %v_ref.1) | copy-start | bytes 786436
  3.7 0.9 %copy-start.3 = (bf16[128,1024]{1,0:T(8,128)(2,1)S(1)}, bf16[128,1024]{1,0:T(8,128)(2,1)}, u32[]{:S(2)}) copy-start(bf16[128,1024]{1,0:T(8,128)(2,1)} %g_ref.1) | copy-start | bytes 786436
where the time goes:
time: 31 us; the launch traced here: 30.8 us
  Pallas kernels  22.4 us (72%)
  local copies, waits for them, and re-layouts  7.68 us (25%)
  between operations  0.7 us (2%)
    pallas_call x1, Pallas kernels, body(): pl.pallas_call(functools.partial(kernel, n, own), out_shape=(grads, grads...  22.4 us
    unnamed x17, local copies, waits for them, and re-layouts  6.08 us
    pallas_call x2, local copies, waits for them, and re-layouts, body(): pl.pallas_call(functools.partial(kernel, n, own), out_shape=(grads, grads...  1.6 us

commit v1 on v0

v1 whole, which is shorter than its diff:
```python
import functools

import jax
import jax.numpy as jnp
from jax import lax
from jax.experimental import pallas as pl
from jax.experimental.pallas import tpu as pltpu
from jax.sharding import PartitionSpec as P

LANES = 128
SUB = 8
MESH = pl.DeviceIdType.MESH
f32 = jnp.float32


def kernel(
    n, own, q_hbm, k_hbm, v_hbm, g_hbm, res_hbm, dec_hbm, skip_hbm,
    conv_out, adj_out, rt_s, dt_s,
    q_ref, k_ref, v_ref, g_ref, res_ref, dec_ref, skip_ref, ins,
    u_s, o_s, conv_s, adj_s, d_s, a_s, w_s,
    ends, got_ends, sums, got_sums, starts, got_starts, totals, got_totals,
    ends_out, ends_in, sums_out, sums_in, starts_out, starts_in, totals_out, totals_in,
):
    rows, cols = q_ref.shape
    modes = res_ref.shape[0]
    groups = cols // LANES
    seq = rows * n
    slab = modes * groups // own
    per = slab // SUB
    me = lax.axis_index("ctx")

    barrier = pltpu.get_barrier_semaphore()
    fetches = [
        pltpu.make_async_copy(src, dst, ins.at[i])
        for i, (src, dst) in enumerate((
            (dec_hbm, dec_ref), (k_hbm, k_ref), (v_hbm, v_ref), (q_hbm, q_ref),
            (g_hbm, g_ref), (res_hbm, res_ref), (skip_hbm, skip_ref)))
    ]
    for fetch in fetches:
        fetch.start()

    @pl.loop(0, n)
    def _(peer):
        @pl.when(peer != me)
        def _():
            pl.semaphore_signal(barrier, inc=1, device_id={"ctx": peer}, device_id_type=MESH)

    for fetch in fetches:
        fetch.wait()
    for g in range(groups):
        lanes = slice(g * LANES, (g + 1) * LANES)
        block = slice(g * rows, (g + 1) * rows)
        u_s[block, :] = k_ref[:, lanes].astype(f32) * v_ref[:, lanes].astype(f32)
        o_s[block, :] = q_ref[:, lanes].astype(f32) * g_ref[:, lanes].astype(f32)
        d = dec_ref[:, lanes]
        d_s[pl.ds(g, modes, stride=groups), :] = d
        a_s[pl.ds(g, modes, stride=groups), :] = jnp.exp(-d)
        w_s[pl.ds(g, modes, stride=groups), :] = res_ref[:, lanes]

    def at(ref, t):
        return ref.at[pl.ds(t, SUB, stride=rows), :]

    def mode_rows(m):
        return pl.ds(pl.multiple_of(m * SUB, SUB), SUB)

    def link(src, dst, sent, landed, peer):
        return pltpu.make_async_remote_copy(
            src_ref=src, dst_ref=dst, send_sem=sent, recv_sem=landed,
            device_id={"ctx": peer}, device_id_type=MESH)

    def each_other(count, act):
        @pl.loop(0, count)
        def _(i):
            @pl.when(i != me)
            def _():
                act(i)

    def ends_to(q):
        return link(ends.at[q], got_ends.at[me], ends_out.at[q], ends_in.at[me], q)

    def ends_from(r):
        return link(ends.at[0], got_ends.at[r], ends_out.at[0], ends_in.at[r], r)

    def sums_to(q):
        return link(sums.at[q], got_sums.at[me], sums_out.at[q], sums_in.at[me], q)

    def sums_from(r):
        return link(sums.at[0], got_sums.at[r], sums_out.at[0], sums_in.at[r], r)

    def starts_to(r):
        return link(starts.at[r], got_starts.at[me], starts_out.at[r], starts_in.at[me], r)

    def starts_from(q):
        return link(starts.at[0], got_starts.at[q], starts_out.at[0], starts_in.at[q], q)

    def totals_to(r):
        return link(totals, got_totals.at[me], totals_out.at[r], totals_in.at[me], r)

    def totals_from(q):
        return link(totals, got_totals.at[q], totals_out.at[0], totals_in.at[q], q)

    zero = jnp.zeros((SUB, LANES), f32)
    batch = 4
    turns = modes // batch
    owners_per = batch // per
    unroll = 8

    def chunk_of(turn):
        return lax.rem(turn + me // owners_per, turns)

    wide = 16

    def edges(c):
        a = [a_s[mode_rows(c * wide + j), :] for j in range(wide)]

        def step(i, carry):
            x, z = [list(s) for s in carry]
            for k in range(unroll):
                t = i * unroll + k
                ut = at(u_s, t)[...]
                ob = at(o_s, rows - 1 - t)[...]
                for j in range(wide):
                    x[j] = a[j] * x[j] + ut
                    z[j] = a[j] * z[j] + ob
            return tuple(x), tuple(z)

        done = lax.fori_loop(0, rows // unroll, step, ((zero,) * wide,) * 2)
        for j in range(wide):
            sub = slice((j % per) * SUB, (j % per + 1) * SUB)
            for f in range(2):
                ends[c * (wide // per) + j // per, f, sub, :] = done[f][j]

    def summarise(turn):
        c = chunk_of(turn)
        a = [a_s[mode_rows(c * batch + j), :] for j in range(batch)]

        def step(i, carry):
            x, y, r, e, z, v = [list(s) for s in carry]
            for k in range(unroll):
                t = i * unroll + k
                ut = at(u_s, t)[...]
                ot = at(o_s, t)[...]
                ob = at(o_s, rows - 1 - t)[...]
                for j in range(batch):
                    y[j] = a[j] * (y[j] + x[j])
                    x[j] = a[j] * x[j] + ut
                    r[j] = r[j] + ot * x[j]
                    e[j] = e[j] + ot * y[j]
                    z[j] = a[j] * z[j] + ob
                    v[j] = a[j] * v[j] + z[j]
            return tuple(tuple(s) for s in (x, y, r, e, z, v))

        x, y, r, e, z, v = lax.fori_loop(
            0, rows // unroll, step, tuple((zero,) * batch for _ in range(6)))
        for j in range(batch):
            q = c * owners_per + j // per
            sub = slice((j % per) * SUB, (j % per + 1) * SUB)
            for f, value in enumerate((y, r, e, v)):
                sums[q, f, sub, :] = value[j]

    def send_chunk(copy, turn):
        for b in range(owners_per):
            q = chunk_of(turn) * owners_per + b

            @pl.when(q != me)
            def _():
                copy(q).start()

    @pl.loop(0, modes // wide)
    def _(c):
        edges(c)

    pl.semaphore_wait(barrier, n - 1)
    each_other(own, lambda q: ends_to(q).start())

    @pl.loop(0, turns)
    def _(turn):
        summarise(turn)
        send_chunk(sums_to, turn)

    def total(terms):
        while len(terms) > 1:
            terms = [x + y for x, y in zip(terms[::2], terms[1::2])]
        return terms[0]

    skip = jnp.concatenate([skip_ref[:, g * LANES:(g + 1) * LANES] for g in range(groups)], axis=0)

    def scan(src, dst, place):
        def step(i, x):
            x = list(x)
            here = [place(i * unroll + k) for k in range(unroll)]
            terms = [at(src, t)[...] for t in here]
            sums = []
            for term in terms:
                x = [a_s[mode_rows(m), :] * x[m] + term for m in range(modes)]
                sums.append(skip * term + total([w_s[mode_rows(m), :] * x[m] for m in range(modes)]))
            for t, value in zip(here, sums):
                at(dst, t)[...] = value
            return tuple(x)

        lax.fori_loop(0, rows // unroll, step, (zero,) * modes)

    def forward(t):
        return t

    def backward(t):
        return rows - 1 - t

    few = n <= 16
    none = jnp.zeros((slab, LANES), f32)

    def owned():
        mine = pl.ds(pl.multiple_of(lax.rem(me, own) * slab, slab), slab)
        d = d_s[mine, :]
        return d, a_s[mine, :], jnp.exp(-float(rows) * d)

    @pl.when(me < own)
    def _():
        _, _, at_end = owned()
        got_ends[me] = ends[me]
        each_other(n, lambda r: ends_from(r).wait_recv())

        def carry_on(i, carry):
            x, z = carry
            r = n - 1 - i
            starts[i, 0] = x
            starts[r, 1] = z
            return at_end * x + got_ends[i, 0], at_end * z + got_ends[r, 1]

        lax.fori_loop(0, n, carry_on, (none, none), unroll=few)
        each_other(n, lambda r: starts_to(r).start())
        got_starts[me] = starts[me]

    scan(u_s, conv_s, forward)
    scan(o_s, adj_s, backward)

    @pl.when(me < own)
    def _():
        d, a, at_end = owned()
        got_sums[me] = sums[me]
        each_other(n, lambda r: sums_from(r).wait_recv())

        def gather(r, carry):
            y, rt, dt = carry
            x, z = starts[r, 0], got_ends[r, 1]
            rt = rt + got_sums[r, 1] + a * (x * z)
            dt = dt + got_sums[r, 2] + a * (got_sums[r, 3] * x + z * y)
            y = at_end * (y + float(rows) * x) + got_sums[r, 0]
            return y, rt, dt

        _, rt, dt = lax.fori_loop(0, n, gather, (none,) * 3, unroll=few)
        totals[0] = rt / seq
        totals[1] = dt * d / seq
        each_other(n, lambda r: totals_to(r).start())
        got_totals[me] = totals[...]

    each_other(own, lambda q: starts_from(q).wait_recv())

    def decay_from(field, src, dst, place):
        def start(m):
            sub = slice((m % per) * SUB, (m % per + 1) * SUB)
            return w_s[mode_rows(m), :] * a_s[mode_rows(m), :] * got_starts[m // per, field, sub, :]

        def step(i, p):
            p = list(p)
            here = [place(i * unroll + k) for k in range(unroll)]
            local = [at(src, t)[...] for t in here]
            sums = []
            for value in local:
                sums.append(value + total(p))
                p = [a_s[mode_rows(m), :] * p[m] for m in range(modes)]
            for t, value in zip(here, sums):
                at(dst, t)[...] = value
            return tuple(p)

        lax.fori_loop(0, rows // unroll, step, tuple(start(m) for m in range(modes)))

    decay_from(0, conv_s, conv_out, forward)
    decay_from(1, adj_s, adj_out, backward)
    each_other(own, lambda q: totals_from(q).wait_recv())
    for q in range(own):
        rt_s[q * slab:(q + 1) * slab, :] = got_totals[q, 0]
        dt_s[q * slab:(q + 1) * slab, :] = got_totals[q, 1]

    each_other(own, lambda q: ends_to(q).wait_send())
    each_other(own, lambda q: sums_to(q).wait_send())

    @pl.when(me < own)
    def _():
        each_other(n, lambda r: starts_to(r).wait_send())
        each_other(n, lambda r: totals_to(r).wait_send())


def finish(
    conv_ref, adj_ref, rt_ref, dt_ref, k_ref, v_ref, g_ref,
    qg_hbm, kg_hbm, vg_hbm, rg_hbm, dg_hbm,
    qg_ref, kg_ref, vg_ref, rg_ref, dg_ref, outs,
):
    rows, cols = k_ref.shape
    modes = rg_ref.shape[0]
    groups = cols // LANES
    stores = [
        pltpu.make_async_copy(src, dst, outs.at[i])
        for i, (src, dst) in enumerate((
            (rg_ref, rg_hbm), (dg_ref, dg_hbm), (qg_ref, qg_hbm), (kg_ref, kg_hbm), (vg_ref, vg_hbm)))
    ]
    for g in range(groups):
        lanes = slice(g * LANES, (g + 1) * LANES)
        rg_ref[:, lanes] = rt_ref[pl.ds(g, modes, stride=groups), :]
        dg_ref[:, lanes] = dt_ref[pl.ds(g, modes, stride=groups), :]
    stores[0].start()
    stores[1].start()
    for g in range(groups):
        lanes = slice(g * LANES, (g + 1) * LANES)
        block = slice(g * rows, (g + 1) * rows)
        qg_ref[:, lanes] = (g_ref[:, lanes].astype(f32) * conv_ref[block, :]).astype(qg_ref.dtype)
    stores[2].start()
    for g in range(groups):
        lanes = slice(g * LANES, (g + 1) * LANES)
        block = slice(g * rows, (g + 1) * rows)
        kg_ref[:, lanes] = (adj_ref[block, :] * v_ref[:, lanes].astype(f32)).astype(kg_ref.dtype)
        vg_ref[:, lanes] = (adj_ref[block, :] * k_ref[:, lanes].astype(f32)).astype(vg_ref.dtype)
    stores[3].start()
    stores[4].start()
    for store in stores:
        store.wait()


def body(n, queries, keys, values, grad_out, residues, decays, skip):
    rows, cols = queries.shape
    modes = residues.shape[1]
    own = min(n, modes)
    slab = modes * cols // LANES // own
    vmem = pl.BlockSpec(memory_space=pltpu.VMEM)
    hbm = pl.BlockSpec(memory_space=pltpu.HBM)
    size = (rows * cols // LANES, LANES)
    held = (modes * cols // LANES, LANES)
    field = pltpu.VMEM(size, f32)
    table = pltpu.VMEM(held, f32)
    gate = pltpu.VMEM((rows, cols), jnp.bfloat16)
    wide = pltpu.VMEM((modes, cols), f32)
    conv, adj, rt, dt = pl.pallas_call(
        functools.partial(kernel, n, own),
        out_shape=tuple(jax.ShapeDtypeStruct(s, f32) for s in (size, size, held, held)),
        in_specs=[hbm] * 7,
        out_specs=(vmem,) * 4,
        scratch_shapes=[
            gate, gate, gate, gate, wide, wide, pltpu.VMEM((1, cols), f32),
            pltpu.SemaphoreType.DMA((7,)),
            field, field, field, field,
            table, table, table,
            pltpu.VMEM((own, 2, slab, LANES), f32),
            pltpu.VMEM((n, 2, slab, LANES), f32),
            pltpu.VMEM((own, 4, slab, LANES), f32),
            pltpu.VMEM((n, 4, slab, LANES), f32),
            pltpu.VMEM((n, 2, slab, LANES), f32),
            pltpu.VMEM((own, 2, slab, LANES), f32),
            pltpu.VMEM((2, slab, LANES), f32),
            pltpu.VMEM((own, 2, slab, LANES), f32),
        ] + [
            pltpu.SemaphoreType.DMA((count,)) for count in (own, n, own, n, n, own, n, own)
        ],
        compiler_params=pltpu.CompilerParams(
            collective_id=0, has_side_effects=True, vmem_limit_bytes=24 * 1024 * 1024
        ),
    )(*[pltpu.with_memory_space_constraint(x, pltpu.HBM) for x in (queries, keys, values, grad_out, residues.T, decays.T, skip.reshape(1, cols))])
    grads = jax.ShapeDtypeStruct((rows, cols), jnp.bfloat16)
    sums = jax.ShapeDtypeStruct((modes, cols), f32)
    qg, kg, vg, rg, dg = pl.pallas_call(
        finish,
        out_shape=(grads, grads, grads, sums, sums),
        in_specs=[vmem] * 7,
        out_specs=(hbm,) * 5,
        scratch_shapes=[gate, gate, gate, wide, wide, pltpu.SemaphoreType.DMA((5,))],
        compiler_params=pltpu.CompilerParams(vmem_limit_bytes=16 * 1024 * 1024),
    )(conv, adj, rt, dt, keys, values, grad_out)
    return qg, kg, vg, rg.T, dg.T


def solution(mesh):
    return jax.shard_map(
        functools.partial(body, mesh.shape["ctx"]),
        mesh=mesh,
        in_specs=(
            P("ctx", "ch"), P("ctx", "ch"), P("ctx", "ch"), P("ctx", "ch"),
            P("ch", None), P("ch", None), P("ch"),
        ),
        out_specs=(P("ctx", "ch"), P("ctx", "ch"), P("ctx", "ch"), P("ch", None), P("ch", None)),
        check_vma=False,
    )
```

time: 31 us -> 20.8 us (0.67)
  local copies, waits for them, and re-layouts: 7.68 us -> 0.01 us
  Pallas kernels: 22.4 us -> 19.9 us
    unnamed x17 -> x6, local copies, waits for them, and re-layouts: 6.08 us -> 0.01 us
    pallas_call x1 -> x2, Pallas kernels: 22.4 us -> 19.9 us  [the longest x1 18.9 us: body(): pl.pallas_call(functools.partial(kernel, n, own), out_shape=tuple((jax.Sh...]
    pallas_call x2 -> x0, local copies, waits for them, and re-layouts: 1.6 us -> none  [body(): pl.pallas_call(functools.partial(kernel, n, own), out_shape=(grads, grads...]
where the time goes in v1:
time: 20.8 us; the launch traced here: 20.6 us
  Pallas kernels  19.9 us (96%)
  between operations  0.69 us (3%)
    pallas_call x1, Pallas kernels, body(): pl.pallas_call(functools.partial(kernel, n, own), out_shape=tuple((jax.Sh...  18.9 us
    pallas_call x1, Pallas kernels, body(): pl.pallas_call(finish, out_shape=(grads, grads, grads, sums, sums), in_sp...  1.01 us

profile of v1, /device:TPU:0, one launch (start us, length us, event | category | flops | bytes accessed | tf_op | source)
XLA Modules:
  0.0 20.6 jit_solution(2249525988674333956)
XLA Ops:
  0.6 0.0 copy-start
  0.6 0.0 copy-start.1
  0.7 0.0 copy-start.2
  0.7 18.9 %shard_map.110 = (f32[1024,128]{1,0:T(8,128)S(1)}, f32[1024,128]{1,0:T(8,128)S(1)}, f32[128,128]{1,0:T(8,128)S(1)}, f32[128,128]{1,0:T(8,128)S(1)}) custom-call(bf16[128,1024]{1,0:T(8,128)(2,1)} %q_hbm.1, bf16[128,1024]{1,0:T(8,128)(2,1)} %k_ref.1, bf16[128,1024]{1,0:T(8,128)(2,1)} %v_ref.1, bf16[128,1024]{1,0:T(8,128)(2,1)} %g_ref.1, f32[16,1024]{1,0:T(8,128)} %bitcast.5, ...), custom_call_target="tpu_custom_call" | custom-call | tf_op jit(solution)/shard_map/pallas_call | solution.py:342
  19.6 0.0 copy-done
  19.6 0.0 copy-done.1
  19.6 0.0 copy-done.2
  19.6 1.0 %shard_map.111 = (bf16[128,1024]{1,0:T(8,128)(2,1)}, bf16[128,1024]{1,0:T(8,128)(2,1)}, bf16[128,1024]{1,0:T(8,128)(2,1)}, f32[16,1024]{1,0:T(8,128)}, f32[16,1024]{1,0:T(8,128)}) custom-call(f32[1024,128]{1,0:T(8,128)S(1)} %get-tuple-element.14.conv_ref, f32[1024,128]{1,0:T(8,128)S(1)} %get-tuple-element.15.adj_ref, ...), custom_call_target="tpu_custom_call" | custom-call | tf_op jit(solution)/shard_map/pallas_call | solution.py:369
Async XLA Ops:
  0.6 18.9 %copy-start = (bf16[128,1024]{1,0:T(8,128)(2,1)S(1)}, bf16[128,1024]{1,0:T(8,128)(2,1)}, u32[]{:S(2)}) copy-start(bf16[128,1024]{1,0:T(8,128)(2,1)} %k_ref.1) | copy-start | bytes 786436
  0.6 18.9 %copy-start.1 = (bf16[128,1024]{1,0:T(8,128)(2,1)S(1)}, bf16[128,1024]{1,0:T(8,128)(2,1)}, u32[]{:S(2)}) copy-start(bf16[128,1024]{1,0:T(8,128)(2,1)} %v_ref.1) | copy-start | bytes 786436
  0.7 18.9 %copy-start.2 = (bf16[128,1024]{1,0:T(8,128)(2,1)S(1)}, bf16[128,1024]{1,0:T(8,128)(2,1)}, u32[]{:S(2)}) copy-start(bf16[128,1024]{1,0:T(8,128)(2,1)} %g_ref.1) | copy-start | bytes 786436

commit v2 on v1

--- a/solution.py
+++ b/solution.py
@@ -103,32 +103,10 @@
     batch = 4
     turns = modes // batch
     owners_per = batch // per
-    unroll = 8
+    unroll = 16
 
     def chunk_of(turn):
         return lax.rem(turn + me // owners_per, turns)
-
-    wide = 16
-
-    def edges(c):
-        a = [a_s[mode_rows(c * wide + j), :] for j in range(wide)]
-
-        def step(i, carry):
-            x, z = [list(s) for s in carry]
-            for k in range(unroll):
-                t = i * unroll + k
-                ut = at(u_s, t)[...]
-                ob = at(o_s, rows - 1 - t)[...]
-                for j in range(wide):
-                    x[j] = a[j] * x[j] + ut
-                    z[j] = a[j] * z[j] + ob
-            return tuple(x), tuple(z)
-
-        done = lax.fori_loop(0, rows // unroll, step, ((zero,) * wide,) * 2)
-        for j in range(wide):
-            sub = slice((j % per) * SUB, (j % per + 1) * SUB)
-            for f in range(2):
-                ends[c * (wide // per) + j // per, f, sub, :] = done[f][j]
 
     def summarise(turn):
         c = chunk_of(turn)
@@ -155,6 +133,8 @@
         for j in range(batch):
             q = c * owners_per + j // per
             sub = slice((j % per) * SUB, (j % per + 1) * SUB)
+            for f, value in enumerate((x, z)):
+                ends[q, f, sub, :] = value[j]
             for f, value in enumerate((y, r, e, v)):
                 sums[q, f, sub, :] = value[j]
 
@@ -166,16 +146,26 @@
             def _():
                 copy(q).start()
 
-    @pl.loop(0, modes // wide)
-    def _(c):
-        edges(c)
+    early = 1
+
+    @pl.loop(0, early)
+    def _(turn):
+        summarise(turn)
 
     pl.semaphore_wait(barrier, n - 1)
-    each_other(own, lambda q: ends_to(q).start())
+
+    @pl.loop(0, early)
+    def _(turn):
+        send_chunk(ends_to, turn)
+
+    if early < turns:
+        @pl.loop(early, turns)
+        def _(turn):
+            summarise(turn)
+            send_chunk(ends_to, turn)
 
     @pl.loop(0, turns)
     def _(turn):
-        summarise(turn)
         send_chunk(sums_to, turn)
 
     def total(terms):
@@ -206,6 +196,7 @@
     def backward(t):
         return rows - 1 - t
 
+    scan(u_s, conv_s, forward)
     few = n <= 16
     none = jnp.zeros((slab, LANES), f32)
 
@@ -231,7 +222,6 @@
         each_other(n, lambda r: starts_to(r).start())
         got_starts[me] = starts[me]
 
-    scan(u_s, conv_s, forward)
     scan(o_s, adj_s, backward)
 
     @pl.when(me < own)

time: 20.8 us -> 20.2 us (0.971)
  Pallas kernels: 19.9 us -> 19.4 us
    pallas_call x1, Pallas kernels: 18.9 us -> 18.3 us  [body(): pl.pallas_call(functools.partial(kernel, n, own), out_shape=tuple((jax.Sh...]
where the time goes in v2:
time: 20.2 us; the launch traced here: 20.1 us
  Pallas kernels  19.4 us (96%)
  between operations  0.69 us (3%)
    pallas_call x1, Pallas kernels, body(): pl.pallas_call(functools.partial(kernel, n, own), out_shape=tuple((jax.Sh...  18.3 us
    pallas_call x1, Pallas kernels, body(): pl.pallas_call(finish, out_shape=(grads, grads, grads, sums, sums), in_sp...  1.01 us

profile of v2, /device:TPU:0, one launch (start us, length us, event | category | flops | bytes accessed | tf_op | source)
XLA Modules:
  0.0 20.1 jit_solution(2055359251873228571)
XLA Ops:
  0.6 0.0 copy-start
  0.6 0.0 copy-start.1
  0.7 0.0 copy-start.2
  0.7 18.3 %shard_map.110 = (f32[1024,128]{1,0:T(8,128)S(1)}, f32[1024,128]{1,0:T(8,128)S(1)}, f32[128,128]{1,0:T(8,128)S(1)}, f32[128,128]{1,0:T(8,128)S(1)}) custom-call(bf16[128,1024]{1,0:T(8,128)(2,1)} %q_hbm.1, bf16[128,1024]{1,0:T(8,128)(2,1)} %k_ref.1, bf16[128,1024]{1,0:T(8,128)(2,1)} %v_ref.1, bf16[128,1024]{1,0:T(8,128)(2,1)} %g_ref.1, f32[16,1024]{1,0:T(8,128)} %bitcast.5, ...), custom_call_target="tpu_custom_call" | custom-call | tf_op jit(solution)/shard_map/pallas_call | solution.py:332
  19.0 0.0 copy-done
  19.0 0.0 copy-done.1
  19.0 0.0 copy-done.2
  19.0 1.0 %shard_map.111 = (bf16[128,1024]{1,0:T(8,128)(2,1)}, bf16[128,1024]{1,0:T(8,128)(2,1)}, bf16[128,1024]{1,0:T(8,128)(2,1)}, f32[16,1024]{1,0:T(8,128)}, f32[16,1024]{1,0:T(8,128)}) custom-call(f32[1024,128]{1,0:T(8,128)S(1)} %get-tuple-element.14.conv_ref, f32[1024,128]{1,0:T(8,128)S(1)} %get-tuple-element.15.adj_ref, ...), custom_call_target="tpu_custom_call" | custom-call | tf_op jit(solution)/shard_map/pallas_call | solution.py:359
Async XLA Ops:
  0.6 18.4 %copy-start = (bf16[128,1024]{1,0:T(8,128)(2,1)S(1)}, bf16[128,1024]{1,0:T(8,128)(2,1)}, u32[]{:S(2)}) copy-start(bf16[128,1024]{1,0:T(8,128)(2,1)} %k_ref.1) | copy-start | bytes 786436
  0.6 18.4 %copy-start.1 = (bf16[128,1024]{1,0:T(8,128)(2,1)S(1)}, bf16[128,1024]{1,0:T(8,128)(2,1)}, u32[]{:S(2)}) copy-start(bf16[128,1024]{1,0:T(8,128)(2,1)} %v_ref.1) | copy-start | bytes 786436
  0.7 18.4 %copy-start.2 = (bf16[128,1024]{1,0:T(8,128)(2,1)S(1)}, bf16[128,1024]{1,0:T(8,128)(2,1)}, u32[]{:S(2)}) copy-start(bf16[128,1024]{1,0:T(8,128)(2,1)} %g_ref.1) | copy-start | bytes 786436
